TPU v7x, 32 devices: a whole 2x2x4 slice. The times are simulated.
32 devices in a mesh: cohort: 2 (over x), region: 16 (over z, y, core).
Axes of the slice: x: 2, y: 2, z: 4, core: 2. Of those that a mesh axis runs over, the one named last changes fastest.
Arguments:
- dosage: bfloat16 [4096, 16384], P('cohort', 'region'), parts along dimension 0, may hold values from 0 to 2, as said below
- eigvec: bfloat16 [16384, 2048], P('region', 'cohort'), parts along dimension 1, may hold values from -1 to 1, as said below
- eigval: float32 [2, 16384], P('cohort', 'region'), parts along dimension 0, may hold values from 64 to 65536
- pheno: bfloat16 [4096, 128], P('cohort'), parts along dimension 0, may hold values from 0 to 1, as said below
Outputs:
- level1_weights: float32 [128, 128], P('region', 'cohort'), parts along dimension 1
There are 2 independent parts, one for each index of `cohort`. A program takes and returns all parts, laid end to end along the dimension named above; each array names one. Nothing has to cross between parts.
Inputs may be any that keep to these rules, and one draw needn't show every extreme that they name: Every entry is a whole dosage 0, 1 or 2. `eigvec`: the rows of each block form an orthonormal basis up to rounding. `pheno`: every entry is 0 or 1.
All inputs are finite; a program needn't handle non-finite values.
Results may differ from a plain program's by a relative error of at most 0.0051.
Values may be sent and summed in bfloat16 or wider, within the bound.
A program may use at most 64 MiB of HBM per device.

v0:
```python
import jax
import jax.numpy as jnp
from jax import lax
from jax.sharding import PartitionSpec as P

NEWTON = 3


EPSILON = 1e-05
HERITABILITY = (0.01, 0.25, 0.75, 0.99)
LEVEL_ONE = 0.03125


def standardize(values):
    values = values.astype(jnp.float32)
    center = jnp.mean(values, axis=0)
    spread = jnp.sqrt(jnp.mean(jnp.square(values - center), axis=0) + EPSILON)
    return ((values - center) / spread).astype(jnp.bfloat16)


def fit_traits(moved, target, total_samples):
    count_traits = moved.shape[1]
    design = jnp.moveaxis(moved, 1, 0).reshape(count_traits, -1, moved.shape[3])
    predictors = design.shape[1]
    level_ridge = LEVEL_ONE * total_samples
    all_weights = jnp.zeros((count_traits, predictors), jnp.float32)
    own_weights = jnp.zeros((count_traits, predictors), jnp.float32)
    identity = jnp.eye(predictors, dtype=jnp.float32)
    for newton_step in range(NEWTON):
        logits = jnp.einsum(
            "kqn,kq->kn",
            design,
            all_weights.astype(jnp.bfloat16),
            preferred_element_type=jnp.float32,
        )
        prob = jax.nn.sigmoid(logits)
        resid = (target - prob).astype(jnp.bfloat16)
        weighted = (design * (prob * (1.0 - prob))[:, None, :]).astype(jnp.bfloat16)
        gram = jnp.einsum("kqn,kpn->kqp", weighted, design, preferred_element_type=jnp.float32)
        grad = jnp.einsum("kqn,kn->kq", design, resid, preferred_element_type=jnp.float32)
        grad = grad - level_ridge * own_weights
        factor = jnp.linalg.cholesky(gram + level_ridge * identity)
        partial_solve = lax.linalg.triangular_solve(
            factor, grad[:, :, None], left_side=True, lower=True
        )
        update = lax.linalg.triangular_solve(
            factor, partial_solve, left_side=True, lower=True, transpose_a=True
        )
        own_weights = own_weights + update[:, :, 0]
        all_weights = own_weights
    return own_weights


def on_device(dosage, eigvec, eigval, pheno):
    samples, width = dosage.shape
    traits = pheno.shape[1]
    regions = lax.axis_size("region")
    ridges = len(HERITABILITY)
    per_device = traits // regions
    shrink = jnp.array([width * (1.0 - value) / value for value in HERITABILITY], jnp.float32)
    std_trait = standardize(pheno)
    std_geno = standardize(dosage)
    cross = lax.dot_general(
        std_geno, std_trait, (((0,), (0,)), ((), ())), preferred_element_type=jnp.float32
    ).astype(jnp.bfloat16)
    rotated = lax.dot_general(
        eigvec, cross, (((0,), (0,)), ((), ())), preferred_element_type=jnp.float32
    )
    scaled = (rotated[:, None, :] / (eigval[0][:, None, None] + shrink[None, :, None])).astype(
        jnp.bfloat16
    )
    ridge = jnp.dot(
        eigvec, scaled.reshape(width, ridges * traits), preferred_element_type=jnp.float32
    ).astype(jnp.bfloat16)
    position = lax.axis_index("region")
    predicted = lax.dot_general(
        ridge, std_geno, (((0,), (1,)), ((), ())), preferred_element_type=jnp.float32
    ).astype(jnp.bfloat16)
    predicted = predicted.reshape(ridges, traits, 1, samples)
    moved = lax.all_to_all(predicted, "region", split_axis=1, concat_axis=2, tiled=True)
    target = lax.dynamic_slice_in_dim(pheno, position * per_device, per_device, 1)
    weights = fit_traits(moved, target.astype(jnp.float32).T, samples)
    return weights


def solution(mesh):
    return jax.shard_map(
        on_device,
        mesh=mesh,
        in_specs=(
            P("cohort", "region"),
            P("region", "cohort"),
            P("cohort", "region"),
            P("cohort", None),
        ),
        out_specs=P("region", "cohort"),
        check_vma=False,
    )
```

profile of v0, /device:TPU:13, one launch (start us, length us, event | category | flops | bytes accessed | tf_op | source)
XLA Modules:
  0.0 363.7 jit_solution(3730043652886165444)
XLA Ops:
  0.0 3.0 convert_reduce_fusion
  3.1 0.5 copy-done.1
  3.6 1.1 fusion.2
  4.8 3.2 fusion.3
  8.6 5.0 %convolution_bitcast_fusion = f32[1024,128]{0,1:T(8,128)} fusion(bf16[1024,1024]{1,0:T(8,128)(2,1)S(1)} %copy-done, bf16[2048,1024]{1,0:T(8,128)(2,1)} %fusion.3, bf16[2048,128]{1,0:T(8,128)(2,1)S(1)} %copy-done.5, f32[128]{0:T(128)S(1)} %add_sqrt_fusion.1, f32[128]{0:T(128)S(1)} %broadcast_multiply_fusion.1), kind=kOutput, calls=%fused_computation.25 | convolution fusion | flops 806486016 | bytes 7341056 | tf_op jit(solution)/shard_map/dot_general | solution.py:66
  13.6 1.2 copy.50
  15.1 4.6 %divide_convert_fusion = bf16[1024,4,128]{2,1,0:T(4,128)(2,1)} fusion(f32[1024,4]{1,0:T(8,128)S(1)} %broadcast_add_fusion, f32[1024,128]{1,0:T(8,128)S(1)} %copy.50), kind=kLoop, calls=%fused_computation.16 | loop fusion | flops 1048576 | bytes 1589248 | tf_op jit(solution)/shard_map/convert_element_type | solution.py:69
  19.7 7.3 %convolution_convert_fusion = bf16[512,2048]{1,0:T(8,128)(2,1)} fusion(bf16[2048,1024]{1,0:T(8,128)(2,1)} %fusion.3, bf16[1024,1024]{1,0:T(8,128)(2,1)S(1)} %copy-done, bf16[128,8,4,128]{3,2,1,0:T(4,128)(2,1)} %bitcast.211), kind=kOutput, calls=%fused_computation.15 | convolution fusion | flops 3222798336 | bytes 9437184 | tf_op jit(solution)/shard_map/dot_general | solution.py:76
  27.0 4.6 %copy.51 = bf16[4,128,1,2048]{3,0,2,1:T(4,128)(2,1)} copy(bf16[4,128,1,2048]{3,1,0,2:T(8,128)(2,1)} %bitcast.210) | data formatting | bytes 4194304 | tf_op jit(solution)/shard_map/reshape | solution.py:79
  31.6 6.7 %all-to-all-start = ((bf16[4,128,1,2048]{3,0,2,1:T(4,128)(2,1)}), bf16[4,128,1,2048]{3,0,2,1:T(4,128)(2,1)}, u32[]{:S(2)}, u32[]{:S(2)}) async-start(bf16[4,128,1,2048]{3,0,2,1:T(4,128)(2,1)} %copy.51), calls=%async_computation | async-start | bytes 4194304 | tf_op jit(solution)/shard_map/all_to_all | solution.py:80
  38.7 47.1 %all-to-all-done = bf16[4,128,1,2048]{3,0,2,1:T(4,128)(2,1)} async-done(((bf16[4,128,1,2048]{3,0,2,1:T(4,128)(2,1)}), bf16[4,128,1,2048]{3,0,2,1:T(4,128)(2,1)}, u32[]{:S(2)}, u32[]{:S(2)}) %all-to-all-start) | async-done | bytes 2097184 | tf_op jit(solution)/shard_map/all_to_all | solution.py:80
  85.8 2.8 copy.52
  88.6 0.4 fusion.76
  89.0 0.9 copy-done.2
  89.9 0.7 fusion.18
  90.9 46.9 %custom-call.15 = f32[8,64,64]{2,1,0:T(8,128)S(1)} custom-call(f32[8,64,64]{2,1,0:T(8,128)S(1)} %fusion.50), custom_call_target="Cholesky" | custom-call | tf_op jit(solution)/shard_map/jit(cholesky)/cholesky | solution.py:42
  138.1 39.3 %custom-call.17 = f32[8,1,64,64]{2,3,1,0:T(8,128)S(1)} custom-call(f32[8,1,64,64]{3,2,1,0:T(8,128)S(1)} %select_bitcast_fusion.2), custom_call_target="InvertDiagBlocksLowerTriangular" | custom-call | tf_op jit(solution)/shard_map/triangular_solve/custom-call.2 | solution.py:46
  177.4 2.4 convolution_bitcast_fusion.4
  180.1 0.5 fusion.48
  180.7 0.4 fusion.74
  181.1 0.8 fusion.21
  182.1 46.9 %custom-call.18 = f32[8,64,64]{2,1,0:T(8,128)S(1)} custom-call(f32[8,64,64]{2,1,0:T(8,128)S(1)} %fusion.46), custom_call_target="Cholesky" | custom-call | tf_op jit(solution)/shard_map/jit(cholesky)/cholesky | solution.py:42
  229.2 39.3 %custom-call.20 = f32[8,1,64,64]{2,3,1,0:T(8,128)S(1)} custom-call(f32[8,1,64,64]{3,2,1,0:T(8,128)S(1)} %select_bitcast_fusion.1), custom_call_target="InvertDiagBlocksLowerTriangular" | custom-call | tf_op jit(solution)/shard_map/triangular_solve/custom-call.2 | solution.py:46
  268.6 2.4 fusion.65
  271.3 0.5 fusion.44
  271.9 0.4 fusion.72
  272.3 0.7 fusion.24
  273.2 47.1 %custom-call.21 = f32[8,64,64]{2,1,0:T(8,128)S(1)} custom-call(f32[8,64,64]{2,1,0:T(8,128)S(1)} %fusion.42), custom_call_target="Cholesky" | custom-call | tf_op jit(solution)/shard_map/jit(cholesky)/cholesky | solution.py:42
  320.6 39.3 %custom-call.23 = f32[8,1,64,64]{2,3,1,0:T(8,128)S(1)} custom-call(f32[8,1,64,64]{3,2,1,0:T(8,128)S(1)} %select_bitcast_fusion), custom_call_target="InvertDiagBlocksLowerTriangular" | custom-call | tf_op jit(solution)/shard_map/triangular_solve/custom-call.2 | solution.py:46
  359.9 2.2 fusion.63
  362.5 0.5 fusion.40
  363.1 0.6 add_bitcast_fusion
  (51 shorter events, 3.7 us)
Async XLA Ops:
  0.0 8.6 %copy-start = (bf16[1024,1024]{1,0:T(8,128)(2,1)S(1)}, bf16[1024,1024]{1,0:T(8,128)(2,1)}, u32[]{:S(2)}) copy-start(bf16[1024,1024]{1,0:T(8,128)(2,1)} %param.11) | copy-start | bytes 6291460
  0.0 3.6 copy-start.1
  4.8 3.2 copy-start.5
  8.6 6.3 %copy-start.6 = (f32[1,1024]{1,0:T(1,128)S(1)}, f32[1,1024]{1,0:T(1,128)}, u32[]{:S(2)}) copy-start(f32[1,1024]{1,0:T(1,128)} %param.12) | copy-start | bytes 12292
  8.6 6.3 %copy-start.7 = (f32[4]{0:T(128)S(1)}, f32[4]{0:T(128)}, u32[]{:S(2)}) copy-start(f32[4]{0:T(128)} %constant.65.clone) | copy-start | bytes 52
  31.6 54.3 %all-to-all-start = ((bf16[4,128,1,2048]{3,0,2,1:T(4,128)(2,1)}), bf16[4,128,1,2048]{3,0,2,1:T(4,128)(2,1)}, u32[]{:S(2)}, u32[]{:S(2)}) async-start(bf16[4,128,1,2048]{3,0,2,1:T(4,128)(2,1)} %copy.51), calls=%async_computation | async-start | bytes 4194304 | tf_op jit(solution)/shard_map/all_to_all | solution.py:80
  88.6 1.4 copy-start.2
  177.4 3.3 copy-start.3
  268.6 3.3 copy-start.4
where the time goes:
time: 364 us
  other arithmetic  273 us (75%)
  waiting for transfers between devices  47.1 us (13%)
  matrix products  25.4 us (7%)
  local copies, waits for them, and re-layouts  10.8 us (3%)
  starting transfers between devices  6.74 us (2%)
    another operation x10, other arithmetic, fit_traits(): factor = jnp.linalg.cholesky(gram + level_ridge * identity)  141 us
    another operation x7, other arithmetic, fit_traits(): lax.linalg.triangular_solve(factor, partial_solve, left_side=True, lower=...  118 us
    all_to_all x1, waiting for transfers between devices, on_device(): lax.all_to_all(predicted, 'region', split_axis=1, concat_axis=2, tiled=True)  47.1 us
    dot_general x1, matrix products, on_device(): lax.dot_general(ridge, std_geno, (((0,), (1,)), ((), ())), preferred_elem...  7.31 us
  transfers between devices with their start and end apart: 1, of which 1 were waited for; matrix products, arithmetic and copies ran while one was open for 0% of the time, Pallas kernels for 0%

commit v1 on v0

v1 whole, which is shorter than its diff:
```python
import functools

import jax
import jax.numpy as jnp
from jax import lax
from jax.experimental import pallas as pl
from jax.experimental.pallas import tpu as pltpu
from jax.sharding import PartitionSpec as P

NEWTON = 3


EPSILON = 1e-05
HERITABILITY = (0.01, 0.25, 0.75, 0.99)
LEVEL_ONE = 0.03125
LANES = 128
ROWS = 8


def standardize(values):
    values = values.astype(jnp.float32)
    center = jnp.mean(values, axis=0)
    spread = jnp.sqrt(jnp.mean(jnp.square(values - center), axis=0) + EPSILON)
    return ((values - center) / spread).astype(jnp.bfloat16)


def pick_column(matrix, column, width):
    lane = lax.broadcasted_iota(jnp.int32, matrix.shape, 1)
    if matrix.shape[1] == LANES:
        return jnp.take_along_axis(matrix, lane // width * width + column, axis=1)
    chosen = jnp.sum(jnp.where(lane == column, matrix, 0.0), axis=1, keepdims=True)
    return jnp.broadcast_to(chosen, matrix.shape)


def eliminate(curve_ref, slope_ref, width):
    groups = curve_ref.shape[0]
    lanes = curve_ref.shape[2]
    row = lax.broadcasted_iota(jnp.int32, (ROWS, lanes), 0)

    def panel(step, carry):
        first = pl.multiple_of(step * ROWS, ROWS)
        curves = [curve_ref[g, pl.ds(first, ROWS), :] for g in range(groups)]
        slopes = [slope_ref[g, pl.ds(first, ROWS), :] for g in range(groups)]
        for j in range(ROWS):
            for g in range(groups):
                column = pick_column(curves[g], first + j, width)
                inverse = 1.0 / column[j : j + 1, :]
                pivot = curves[g][j : j + 1, :] * inverse
                right = slopes[g][j : j + 1, :] * inverse
                curves[g] = jnp.where(row == j, pivot, curves[g] - column * pivot)
                slopes[g] = jnp.where(row == j, right, slopes[g] - column * right)
        for g in range(groups):
            old = curve_ref[g]
            curve = old
            slope = slope_ref[g]
            for j in range(ROWS):
                column = pick_column(old, first + j, width)
                curve = curve - column * curves[g][j : j + 1, :]
                slope = slope - column * slopes[g][j : j + 1, :]
            curve_ref[g] = curve
            slope_ref[g] = slope
        for g in range(groups):
            curve_ref[g, pl.ds(first, ROWS), :] = curves[g]
            slope_ref[g, pl.ds(first, ROWS), :] = slopes[g]
        return carry

    lax.fori_loop(0, width // ROWS, panel, 0)


def spread_weights(weight_ref, chunk, width, count, pack):
    lane = lax.broadcasted_iota(jnp.int32, (width, LANES), 1)
    parts = []
    for t in range(count):
        group, half = divmod(chunk * count + t, pack)
        held = weight_ref[group][:, :LANES]
        if half:
            held = pltpu.roll(held, LANES - half * width, 1)
        parts.append(jnp.where(lane == t, held, 0.0))
    return jnp.concatenate(parts, axis=0).T[:ROWS, :]


def fit_kernel(width, design_ref, target_ref, out_ref, curve_ref, slope_ref, weight_ref):
    chunks, rows, samples = design_ref.shape
    count = rows // width
    lanes = curve_ref.shape[2]
    pack = lanes // width
    tile = 512
    ridge = LEVEL_ONE * samples
    weight_ref[...] = jnp.zeros_like(weight_ref)
    lane = lax.broadcasted_iota(jnp.int32, (width, lanes), 1)
    row = lax.broadcasted_iota(jnp.int32, (width, lanes), 0)
    identity = jnp.where(lane % width == row, ridge, 0.0)

    def newton(step, carry):
        for chunk in range(chunks):
            weights = spread_weights(weight_ref, chunk, width, count, pack).astype(jnp.bfloat16)
            gram = jnp.zeros((rows, rows), jnp.float32)
            grad = jnp.zeros((rows, ROWS), jnp.float32)
            for first in range(0, samples, tile):
                design = design_ref[chunk, :, first : first + tile]
                logits = jnp.dot(weights, design, preferred_element_type=jnp.float32)
                prob = 1.0 / (1.0 + jnp.exp(-logits))
                resid = (target_ref[chunk, :, first : first + tile] - prob).astype(jnp.bfloat16)
                curve = prob * (1.0 - prob)
                weighted = jnp.concatenate(
                    [
                        (
                            design[t * width : (t + 1) * width].astype(jnp.float32)
                            * curve[t : t + 1, :]
                        ).astype(jnp.bfloat16)
                        for t in range(count)
                    ],
                    axis=0,
                )
                last = (((1,), (1,)), ((), ()))
                gram += lax.dot_general(weighted, design, last, preferred_element_type=jnp.float32)
                grad += lax.dot_general(design, resid, last, preferred_element_type=jnp.float32)
            for own in range(count // pack):
                group = chunk * count // pack + own
                curve = None
                for half in range(pack):
                    t = own * pack + half
                    part = gram[t * width : (t + 1) * width, own * lanes : (own + 1) * lanes]
                    side = jnp.broadcast_to(
                        grad[t * width : (t + 1) * width, t : t + 1], (width, lanes)
                    )
                    if curve is None:
                        curve, slope = part, side
                    else:
                        curve = jnp.where(lane < half * width, curve, part)
                        slope = jnp.where(lane < half * width, slope, side)
                curve_ref[group] = curve + identity
                slope_ref[group] = slope - ridge * weight_ref[group]
        eliminate(curve_ref, slope_ref, width)
        weight_ref[...] += slope_ref[...]
        return carry

    lax.fori_loop(0, NEWTON, newton, 0)
    for chunk in range(chunks):
        out_ref[chunk] = spread_weights(weight_ref, chunk, width, count, pack)


def fit_traits(moved, target):
    traits, samples = target.shape
    design = jnp.moveaxis(moved, 1, 0).reshape(traits, -1, samples)
    width = design.shape[1]
    lanes = max(width, LANES)
    count = max(1, 2 * LANES // width)
    chunks = traits // count
    groups = traits * width // lanes
    target = jnp.pad(
        target.reshape(chunks, count, samples), ((0, 0), (0, ROWS - count), (0, 0))
    )
    weights = pl.pallas_call(
        functools.partial(fit_kernel, width),
        out_shape=jax.ShapeDtypeStruct((chunks, ROWS, count * width), jnp.float32),
        in_specs=[pl.BlockSpec(memory_space=pltpu.VMEM)] * 2,
        out_specs=pl.BlockSpec(memory_space=pltpu.VMEM),
        scratch_shapes=[pltpu.VMEM((groups, width, lanes), jnp.float32)] * 3,
        compiler_params=pltpu.CompilerParams(vmem_limit_bytes=48 * 2**20),
        name="newton",
    )(design.reshape(chunks, count * width, samples), target)
    return jnp.sum(weights, axis=1).reshape(traits, width)


def on_device(dosage, eigvec, eigval, pheno):
    samples, width = dosage.shape
    traits = pheno.shape[1]
    regions = lax.axis_size("region")
    ridges = len(HERITABILITY)
    per_device = traits // regions
    shrink = jnp.array([width * (1.0 - value) / value for value in HERITABILITY], jnp.float32)
    std_trait = standardize(pheno)
    std_geno = standardize(dosage)
    cross = lax.dot_general(
        std_geno, std_trait, (((0,), (0,)), ((), ())), preferred_element_type=jnp.float32
    ).astype(jnp.bfloat16)
    rotated = lax.dot_general(
        eigvec, cross, (((0,), (0,)), ((), ())), preferred_element_type=jnp.float32
    )
    scaled = (rotated[:, None, :] / (eigval[0][:, None, None] + shrink[None, :, None])).astype(
        jnp.bfloat16
    )
    ridge = jnp.dot(
        eigvec, scaled.reshape(width, ridges * traits), preferred_element_type=jnp.float32
    ).astype(jnp.bfloat16)
    position = lax.axis_index("region")
    predicted = lax.dot_general(
        ridge, std_geno, (((0,), (1,)), ((), ())), preferred_element_type=jnp.float32
    ).astype(jnp.bfloat16)
    predicted = predicted.reshape(ridges, traits, 1, samples)
    moved = lax.all_to_all(predicted, "region", split_axis=1, concat_axis=2, tiled=True)
    target = lax.dynamic_slice_in_dim(pheno, position * per_device, per_device, 1)
    return fit_traits(moved, target.astype(jnp.float32).T)


def solution(mesh):
    return jax.shard_map(
        on_device,
        mesh=mesh,
        in_specs=(
            P("cohort", "region"),
            P("region", "cohort"),
            P("cohort", "region"),
            P("cohort", None),
        ),
        out_specs=P("region", "cohort"),
        check_vma=False,
    )
```

time: 364 us -> 119 us (0.33)
  other arithmetic: 273 us -> 12.8 us
  Pallas kernels: 0 us -> 27.9 us
  matrix products: 25.4 us -> 12.3 us
    another operation x17 -> x0, other arithmetic: 260 us -> none  [the longest x10 141 us: fit_traits(): factor = jnp.linalg.cholesky(gram + level_ridge * identity)]
    pallas_call x0 -> x1, Pallas kernels: none -> 27.9 us  [fit_traits(): pl.pallas_call(functools.partial(fit_kernel, width), out_shape=jax.ShapeD...]
    dot_general x9 -> x0, matrix products: 10.4 us -> none  [the longest x3 7.01 us: fit_traits(): jnp.einsum('kqn,kn->kq', design, resid, preferred_element_type=jnp.float32)]
where the time goes in v1:
time: 119 us; the launch traced here: 118 us
  waiting for transfers between devices  47.1 us (40%)
  Pallas kernels  27.9 us (23%)
  other arithmetic  12.8 us (11%)
  matrix products  12.3 us (10%)
  local copies, waits for them, and re-layouts  11.3 us (9%)
  starting transfers between devices  6.74 us (6%)
    all_to_all x1, waiting for transfers between devices, on_device(): lax.all_to_all(predicted, 'region', split_axis=1, concat_axis=2, tiled=True)  47.1 us
    pallas_call x1, Pallas kernels, fit_traits(): pl.pallas_call(functools.partial(fit_kernel, width), out_shape=jax.ShapeD...  27.9 us
    dot_general x1, matrix products, on_device(): lax.dot_general(ridge, std_geno, (((0,), (1,)), ((), ())), preferred_elem...  7.31 us
    all_to_all x1, starting transfers between devices, on_device(): lax.all_to_all(predicted, 'region', split_axis=1, concat_axis=2, tiled=True)  6.74 us
    dot_general x1, matrix products, on_device(): lax.dot_general(eigvec, cross, (((0,), (0,)), ((), ())), preferred_elemen...  5.03 us
    convert_element_type x1, other arithmetic, on_device(): (rotated[:, None, :] / (eigval[0][:, None, None] + shrink[None, :, None])...  4.59 us
    reshape x1, local copies, waits for them, and re-layouts, on_device(): predicted = predicted.reshape(ridges, traits, 1, samples)  4.56 us
    reduce_sum x2, other arithmetic, standardize(): center = jnp.mean(values, axis=0)  3.33 us
  transfers between devices with their start and end apart: 1, of which 1 were waited for; matrix products, arithmetic and copies ran while one was open for 0% of the time, Pallas kernels for 0%

profile of v1, /device:TPU:13, one launch (start us, length us, event | category | flops | bytes accessed | tf_op | source)
XLA Modules:
  0.0 118.3 jit_solution(12348978669720254283)
XLA Ops:
  0.0 0.0 copy-start
  0.0 0.0 copy-start.1
  0.0 3.0 %convert_reduce_fusion = f32[1024]{0:T(1024)S(1)} fusion(bf16[2048,1024]{1,0:T(8,128)(2,1)} %param.5), kind=kLoop, calls=%fused_computation.1 | loop fusion | flops 4193280 | bytes 4198400 | tf_op jit(solution)/shard_map/reduce_sum | solution.py:22
  3.1 0.5 copy-done.1
  3.6 1.1 fusion.2
  4.8 0.0 copy-start.2
  4.8 3.2 %fusion.3 = bf16[2048,1024]{1,0:T(8,128)(2,1)} fusion(bf16[2048,1024]{1,0:T(8,128)(2,1)S(1)} %copy-done.1, f32[1024]{0:T(1024)S(1)} %add_sqrt_fusion, f32[1024]{0:T(1024)S(1)} %broadcast_multiply_fusion), kind=kLoop, calls=%fused_computation.5 | loop fusion | flops 8388608 | bytes 8396800 | tf_op jit(solution)/shard_map/convert_element_type | solution.py:24
  8.0 0.0 copy-done.2
  8.0 0.3 convert_reduce_fusion.1
  8.3 0.3 fusion.6
  8.6 0.0 copy-done
  8.6 0.0 copy-start.3
  8.6 0.0 copy-start.4
  8.6 5.0 %convolution_bitcast_fusion = f32[1024,128]{0,1:T(8,128)} fusion(bf16[1024,1024]{1,0:T(8,128)(2,1)S(1)} %copy-done, bf16[2048,1024]{1,0:T(8,128)(2,1)} %fusion.3, bf16[2048,128]{1,0:T(8,128)(2,1)S(1)} %copy-done.2, f32[128]{0:T(128)S(1)} %add_sqrt_fusion.1, f32[128]{0:T(128)S(1)} %broadcast_multiply_fusion.1), kind=kOutput, calls=%fused_computation.14 | convolution fusion | flops 806486016 | bytes 7341056 | tf_op jit(solution)/shard_map/dot_general | solution.py:178
  13.6 1.2 %copy.11 = f32[1024,128]{1,0:T(8,128)S(1)} copy(f32[1024,128]{0,1:T(8,128)} %convolution_bitcast_fusion) | data formatting | bytes 1048576 | tf_op jit(solution)/shard_map/dot_general | solution.py:178
  14.9 0.0 copy-done.3
  14.9 0.0 copy-done.4
  14.9 0.2 broadcast_add_fusion
  15.1 4.6 %divide_convert_fusion = bf16[1024,4,128]{2,1,0:T(4,128)(2,1)} fusion(f32[1024,4]{1,0:T(8,128)S(1)} %broadcast_add_fusion, f32[1024,128]{1,0:T(8,128)S(1)} %copy.11), kind=kLoop, calls=%fused_computation.7 | loop fusion | flops 1048576 | bytes 1589248 | tf_op jit(solution)/shard_map/convert_element_type | solution.py:181
  19.7 7.3 %convolution_convert_fusion = bf16[512,2048]{1,0:T(8,128)(2,1)} fusion(bf16[2048,1024]{1,0:T(8,128)(2,1)} %fusion.3, bf16[1024,1024]{1,0:T(8,128)(2,1)S(1)} %copy-done, bf16[128,8,4,128]{3,2,1,0:T(4,128)(2,1)} %bitcast.29), kind=kOutput, calls=%fused_computation.6 | convolution fusion | flops 3222798336 | bytes 9437184 | tf_op jit(solution)/shard_map/dot_general | solution.py:188
  27.0 4.6 %copy.12 = bf16[4,128,1,2048]{3,0,2,1:T(4,128)(2,1)} copy(bf16[4,128,1,2048]{3,1,0,2:T(8,128)(2,1)} %bitcast.28) | data formatting | bytes 4194304 | tf_op jit(solution)/shard_map/reshape | solution.py:191
  31.6 6.7 %all-to-all-start = ((bf16[4,128,1,2048]{3,0,2,1:T(4,128)(2,1)}), bf16[4,128,1,2048]{3,0,2,1:T(4,128)(2,1)}, u32[]{:S(2)}, u32[]{:S(2)}) async-start(bf16[4,128,1,2048]{3,0,2,1:T(4,128)(2,1)} %copy.12), calls=%async_computation | async-start | bytes 4194304 | tf_op jit(solution)/shard_map/all_to_all | solution.py:192
  38.3 0.2 dynamic-slice_bitcast_fusion
  38.5 0.2 copy.15
  38.7 47.1 %all-to-all-done = bf16[4,128,1,2048]{3,0,2,1:T(4,128)(2,1)} async-done(((bf16[4,128,1,2048]{3,0,2,1:T(4,128)(2,1)}), bf16[4,128,1,2048]{3,0,2,1:T(4,128)(2,1)}, u32[]{:S(2)}, u32[]{:S(2)}) %all-to-all-start) | async-done | bytes 2097184 | tf_op jit(solution)/shard_map/all_to_all | solution.py:192
  85.8 2.7 %copy.24 = bf16[4,128,1,2048]{3,1,0,2:T(8,128)(2,1)S(1)} copy(bf16[4,128,1,2048]{3,0,2,1:T(4,128)(2,1)} %all-to-all-done) | data formatting | bytes 4194304 | tf_op jit(solution)/shard_map/all_to_all | solution.py:192
  88.6 1.2 copy.14
  89.7 27.9 %newton.1 = f32[2,8,256]{2,1,0:T(8,128)S(1)} custom-call(bf16[2,256,2048]{2,1,0:T(8,128)(2,1)S(1)} %bitcast.26, f32[2,8,2048]{2,1,0:T(8,128)S(1)} %pad_convert_fusion.target_ref), custom_call_target="tpu_custom_call" | custom-call | tf_op jit(solution)/shard_map/newton/pallas_call | solution.py:154
  117.6 0.7 reshape.69
  (7 shorter events, 0.1 us)
Async XLA Ops:
  0.0 8.6 %copy-start = (bf16[1024,1024]{1,0:T(8,128)(2,1)S(1)}, bf16[1024,1024]{1,0:T(8,128)(2,1)}, u32[]{:S(2)}) copy-start(bf16[1024,1024]{1,0:T(8,128)(2,1)} %param.6) | copy-start | bytes 6291460
  0.0 3.6 %copy-start.1 = (bf16[2048,1024]{1,0:T(8,128)(2,1)S(1)}, bf16[2048,1024]{1,0:T(8,128)(2,1)}, u32[]{:S(2)}) copy-start(bf16[2048,1024]{1,0:T(8,128)(2,1)} %param.5) | copy-start | bytes 12582916
  4.8 3.2 %copy-start.2 = (bf16[2048,128]{1,0:T(8,128)(2,1)S(1)}, bf16[2048,128]{1,0:T(8,128)(2,1)}, u32[]{:S(2)}) copy-start(bf16[2048,128]{1,0:T(8,128)(2,1)} %param.8) | copy-start | bytes 1572868
  8.6 6.3 %copy-start.3 = (f32[1,1024]{1,0:T(1,128)S(1)}, f32[1,1024]{1,0:T(1,128)}, u32[]{:S(2)}) copy-start(f32[1,1024]{1,0:T(1,128)} %param.7) | copy-start | bytes 12292
  8.6 6.3 %copy-start.4 = (f32[4]{0:T(128)S(1)}, f32[4]{0:T(128)}, u32[]{:S(2)}) copy-start(f32[4]{0:T(128)} %constant.27.clone) | copy-start | bytes 52
  31.6 54.3 %all-to-all-start = ((bf16[4,128,1,2048]{3,0,2,1:T(4,128)(2,1)}), bf16[4,128,1,2048]{3,0,2,1:T(4,128)(2,1)}, u32[]{:S(2)}, u32[]{:S(2)}) async-start(bf16[4,128,1,2048]{3,0,2,1:T(4,128)(2,1)} %copy.12), calls=%async_computation | async-start | bytes 4194304 | tf_op jit(solution)/shard_map/all_to_all | solution.py:192

commit v2 on v1

--- a/solution.py
+++ b/solution.py
@@ -15,13 +15,6 @@
 LEVEL_ONE = 0.03125
 LANES = 128
 ROWS = 8
-
-
-def standardize(values):
-    values = values.astype(jnp.float32)
-    center = jnp.mean(values, axis=0)
-    spread = jnp.sqrt(jnp.mean(jnp.square(values - center), axis=0) + EPSILON)
-    return ((values - center) / spread).astype(jnp.bfloat16)
 
 
 def pick_column(matrix, column, width):
@@ -79,7 +72,7 @@
     return jnp.concatenate(parts, axis=0).T[:ROWS, :]
 
 
-def fit_kernel(width, design_ref, target_ref, out_ref, curve_ref, slope_ref, weight_ref):
+def fit(width, target_chunk, design_ref, target_ref, curve_ref, slope_ref, weight_ref):
     chunks, rows, samples = design_ref.shape
     count = rows // width
     lanes = curve_ref.shape[2]
@@ -100,7 +93,8 @@
                 design = design_ref[chunk, :, first : first + tile]
                 logits = jnp.dot(weights, design, preferred_element_type=jnp.float32)
                 prob = 1.0 / (1.0 + jnp.exp(-logits))
-                resid = (target_ref[chunk, :, first : first + tile] - prob).astype(jnp.bfloat16)
+                target = target_ref[target_chunk + chunk, :, first : first + tile]
+                resid = (target - prob).astype(jnp.bfloat16)
                 curve = prob * (1.0 - prob)
                 weighted = jnp.concatenate(
                     [
@@ -112,9 +106,8 @@
                     ],
                     axis=0,
                 )
-                last = (((1,), (1,)), ((), ()))
-                gram += lax.dot_general(weighted, design, last, preferred_element_type=jnp.float32)
-                grad += lax.dot_general(design, resid, last, preferred_element_type=jnp.float32)
+                gram += dot_last(weighted, design)
+                grad += dot_last(design, resid)
             for own in range(count // pack):
                 group = chunk * count // pack + own
                 curve = None
@@ -136,62 +129,245 @@
         return carry
 
     lax.fori_loop(0, NEWTON, newton, 0)
-    for chunk in range(chunks):
-        out_ref[chunk] = spread_weights(weight_ref, chunk, width, count, pack)
-
-
-def fit_traits(moved, target):
-    traits, samples = target.shape
-    design = jnp.moveaxis(moved, 1, 0).reshape(traits, -1, samples)
-    width = design.shape[1]
-    lanes = max(width, LANES)
-    count = max(1, 2 * LANES // width)
-    chunks = traits // count
-    groups = traits * width // lanes
-    target = jnp.pad(
-        target.reshape(chunks, count, samples), ((0, 0), (0, ROWS - count), (0, 0))
+
+
+def dot_last(left, right):
+    return lax.dot_general(
+        left, right, (((1,), (1,)), ((), ())), preferred_element_type=jnp.float32
     )
-    weights = pl.pallas_call(
-        functools.partial(fit_kernel, width),
-        out_shape=jax.ShapeDtypeStruct((chunks, ROWS, count * width), jnp.float32),
-        in_specs=[pl.BlockSpec(memory_space=pltpu.VMEM)] * 2,
-        out_specs=pl.BlockSpec(memory_space=pltpu.VMEM),
-        scratch_shapes=[pltpu.VMEM((groups, width, lanes), jnp.float32)] * 3,
-        compiler_params=pltpu.CompilerParams(vmem_limit_bytes=48 * 2**20),
-        name="newton",
-    )(design.reshape(chunks, count * width, samples), target)
-    return jnp.sum(weights, axis=1).reshape(traits, width)
+
+
+def kernel(
+    regions,
+    dosage_ref,
+    eigvec_ref,
+    eigval_ref,
+    pheno_ref,
+    out_ref,
+    geno_ref,
+    trait_ref,
+    std_trait_ref,
+    cross_ref,
+    wide_ref,
+    scaled_ref,
+    ridge_ref,
+    sent_ref,
+    held_ref,
+    design_ref,
+    target_ref,
+    curve_ref,
+    slope_ref,
+    weight_ref,
+    send_sem,
+    recv_sem,
+):
+    samples, block = dosage_ref.shape
+    traits = pheno_ref.shape[1]
+    sends, _, piece, _ = sent_ref.shape
+    chunks, rows, _ = design_ref.shape
+    ridges = len(HERITABILITY)
+    width = regions * ridges
+    count = rows // width
+    per_device = traits // regions
+    per_send = per_device // sends
+    tile = 256
+    me = lax.axis_index("region")
+
+    barrier = pltpu.get_barrier_semaphore()
+
+    def greet(k, carry):
+        other = lax.rem(me + k, regions)
+        pl.semaphore_signal(
+            barrier, inc=1, device_id={"region": other}, device_id_type=pl.DeviceIdType.MESH
+        )
+        return carry
+
+    lax.fori_loop(1, regions, greet, 0)
+    pl.semaphore_wait(barrier, regions - 1)
+
+    trait = pheno_ref[...].astype(jnp.float32).T
+    trait_ref[...] = trait
+    center = jnp.mean(trait, axis=1, keepdims=True)
+    spread = jnp.sqrt(jnp.mean(jnp.square(trait - center), axis=1, keepdims=True) + EPSILON)
+    std_trait_ref[...] = ((trait - center) / spread).astype(jnp.bfloat16)
+    target_ref[...] = jnp.zeros_like(target_ref)
+    for t in range(per_device):
+        target_ref[t // count, t % count : t % count + 1, :] = trait_ref[
+            pl.ds(me * per_device + t, 1), :
+        ]
+
+    def totals(i, carry):
+        first, second = carry
+        part = dosage_ref[pl.ds(pl.multiple_of(i * tile, tile), tile), :].astype(jnp.float32)
+        part = part.reshape(tile // ROWS, ROWS, block)
+        return first + jnp.sum(part, axis=0), second + jnp.sum(part * part, axis=0)
+
+    zero = jnp.zeros((ROWS, block), jnp.float32)
+    first, second = lax.fori_loop(0, samples // tile, totals, (zero, zero))
+    first = jnp.sum(first, axis=0, keepdims=True)
+    second = jnp.sum(second, axis=0, keepdims=True)
+    mean = first / samples
+    variance = (samples * second - first * first) / (samples * samples)
+    scale = 1.0 / jnp.sqrt(variance + EPSILON)
+    cross_ref[...] = jnp.zeros_like(cross_ref)
+
+    def normalize(i, carry):
+        here = pl.ds(pl.multiple_of(i * tile, tile), tile)
+        part = ((dosage_ref[here, :].astype(jnp.float32) - mean) * scale).astype(jnp.bfloat16)
+        geno_ref[here, :] = part
+        cross_ref[...] += jnp.dot(
+            std_trait_ref[:, here], part, preferred_element_type=jnp.float32
+        )
+        return carry
+
+    lax.fori_loop(0, samples // tile, normalize, 0)
+
+    all_rows = traits * ridges
+    place = lax.broadcasted_iota(jnp.int32, (all_rows, traits), 0)
+    which = lax.broadcasted_iota(jnp.int32, (all_rows, traits), 1)
+    source = (
+        place // piece % regions * per_device
+        + place // (piece * regions) * per_send
+        + place % per_send
+    )
+    choose = jnp.where(source == which, 1.0, 0.0).astype(jnp.bfloat16)
+    wide_ref[...] = jnp.dot(
+        choose, cross_ref[...].astype(jnp.bfloat16), preferred_element_type=jnp.float32
+    ).astype(jnp.bfloat16)
+    kind = lax.broadcasted_iota(jnp.int32, (all_rows, tile), 0) // per_send % ridges
+    shrink = jnp.zeros((all_rows, tile), jnp.float32)
+    for r, value in enumerate(HERITABILITY):
+        shrink = jnp.where(kind == r, block * (1.0 - value) / value, shrink)
+
+    def rotate(i, carry):
+        here = pl.ds(pl.multiple_of(i * tile, tile), tile)
+        rotated = jnp.dot(wide_ref[...], eigvec_ref[:, here], preferred_element_type=jnp.float32)
+        scaled_ref[:, here] = (rotated / (eigval_ref[:, here] + shrink)).astype(jnp.bfloat16)
+        return carry
+
+    lax.fori_loop(0, block // tile, rotate, 0)
+
+    def back(i, carry):
+        here = pl.ds(pl.multiple_of(i * tile, tile), tile)
+        ridge_ref[:, here] = dot_last(scaled_ref[...], eigvec_ref[here, :]).astype(jnp.bfloat16)
+        return carry
+
+    lax.fori_loop(0, block // tile, back, 0)
+
+    def copy(send, other, slot):
+        return pltpu.make_async_remote_copy(
+            src_ref=sent_ref.at[send, other],
+            dst_ref=held_ref.at[send, slot],
+            send_sem=send_sem.at[send, other],
+            recv_sem=recv_sem.at[send, slot],
+            device_id={"region": other},
+            device_id_type=pl.DeviceIdType.MESH,
+        )
+
+    send_rows = regions * piece
+    for send in range(sends):
+
+        def predict(i, carry):
+            here = pl.ds(pl.multiple_of(i * tile, tile), tile)
+            part = dot_last(
+                ridge_ref[send * send_rows : (send + 1) * send_rows, :], geno_ref[here, :]
+            )
+            part = part.astype(jnp.bfloat16).astype(sent_ref.dtype)
+            sent_ref[send, :, :, here] = part.reshape(regions, piece, tile)
+            return carry
+
+        lax.fori_loop(0, samples // tile, predict, 0)
+
+        def start(k, carry):
+            offset = regions // 2 + (k + 1) // 2 * (1 - 2 * (k % 2))
+            copy(send, lax.rem(me + offset, regions), me).start()
+            return carry
+
+        lax.fori_loop(0, regions - 1, start, 0)
+        held_ref[send, me] = sent_ref[send, me]
+
+    place = lax.broadcasted_iota(jnp.int32, (send_rows, send_rows), 0)
+    which = lax.broadcasted_iota(jnp.int32, (send_rows, send_rows), 1)
+    wanted = which % per_send * width + which // per_send % ridges * regions + which // piece
+    order = jnp.where(place == wanted, 1.0, 0.0).astype(jnp.bfloat16)
+    for send in range(sends):
+
+        def arrive(k, carry):
+            other = lax.rem(me + k, regions)
+            copy(send, other, other).wait_recv()
+            return carry
+
+        lax.fori_loop(1, regions, arrive, 0)
+
+        def sort(i, carry):
+            here = pl.ds(pl.multiple_of(i * tile, tile), tile)
+            part = held_ref[send, :, :, here].reshape(send_rows, tile).astype(jnp.bfloat16)
+            part = jnp.dot(order, part, preferred_element_type=jnp.float32).astype(jnp.bfloat16)
+            design_ref[:, :, here] = part.reshape(chunks, rows, tile)
+            return carry
+
+        lax.fori_loop(0, samples // tile, sort, 0)
+        fit(width, send * chunks, design_ref, target_ref, curve_ref, slope_ref, weight_ref)
+        for chunk in range(chunks):
+            out_ref[send * chunks + chunk] = spread_weights(
+                weight_ref, chunk, width, count, curve_ref.shape[2] // width
+            )
+
+    for send in range(sends):
+
+        def leave(k, carry):
+            other = lax.rem(me + k, regions)
+            copy(send, other, other).wait_send()
+            return carry
+
+        lax.fori_loop(1, regions, leave, 0)
 
 
 def on_device(dosage, eigvec, eigval, pheno):
-    samples, width = dosage.shape
+    samples, block = dosage.shape
     traits = pheno.shape[1]
     regions = lax.axis_size("region")
     ridges = len(HERITABILITY)
     per_device = traits // regions
-    shrink = jnp.array([width * (1.0 - value) / value for value in HERITABILITY], jnp.float32)
-    std_trait = standardize(pheno)
-    std_geno = standardize(dosage)
-    cross = lax.dot_general(
-        std_geno, std_trait, (((0,), (0,)), ((), ())), preferred_element_type=jnp.float32
-    ).astype(jnp.bfloat16)
-    rotated = lax.dot_general(
-        eigvec, cross, (((0,), (0,)), ((), ())), preferred_element_type=jnp.float32
-    )
-    scaled = (rotated[:, None, :] / (eigval[0][:, None, None] + shrink[None, :, None])).astype(
-        jnp.bfloat16
-    )
-    ridge = jnp.dot(
-        eigvec, scaled.reshape(width, ridges * traits), preferred_element_type=jnp.float32
-    ).astype(jnp.bfloat16)
-    position = lax.axis_index("region")
-    predicted = lax.dot_general(
-        ridge, std_geno, (((0,), (1,)), ((), ())), preferred_element_type=jnp.float32
-    ).astype(jnp.bfloat16)
-    predicted = predicted.reshape(ridges, traits, 1, samples)
-    moved = lax.all_to_all(predicted, "region", split_axis=1, concat_axis=2, tiled=True)
-    target = lax.dynamic_slice_in_dim(pheno, position * per_device, per_device, 1)
-    return fit_traits(moved, target.astype(jnp.float32).T)
+    width = regions * ridges
+    lanes = max(width, LANES)
+    count = max(1, 2 * LANES // width)
+    per_send = max(count, min(per_device, 2))
+    sends = per_device // per_send
+    chunks = per_send // count
+    groups = per_send * width // lanes
+    piece = per_send * ridges
+    wire = jnp.bfloat16 if piece % 16 == 0 else jnp.float32
+    vmem = pltpu.VMEM
+    weights = pl.pallas_call(
+        functools.partial(kernel, regions),
+        out_shape=jax.ShapeDtypeStruct((sends * chunks, ROWS, count * width), jnp.float32),
+        in_specs=[pl.BlockSpec(memory_space=vmem)] * 4,
+        out_specs=pl.BlockSpec(memory_space=vmem),
+        scratch_shapes=[
+            vmem((samples, block), jnp.bfloat16),
+            vmem((traits, samples), jnp.float32),
+            vmem((traits, samples), jnp.bfloat16),
+            vmem((traits, block), jnp.float32),
+            vmem((traits * ridges, block), jnp.bfloat16),
+            vmem((traits * ridges, block), jnp.bfloat16),
+            vmem((traits * ridges, block), jnp.bfloat16),
+            vmem((sends, regions, piece, samples), wire),
+            vmem((sends, regions, piece, samples), wire),
+            vmem((chunks, count * width, samples), jnp.bfloat16),
+            vmem((sends * chunks, ROWS, samples), jnp.float32),
+            vmem((groups, width, lanes), jnp.float32),
+            vmem((groups, width, lanes), jnp.float32),
+            vmem((groups, width, lanes), jnp.float32),
+            pltpu.SemaphoreType.DMA((sends, regions)),
+            pltpu.SemaphoreType.DMA((sends, regions)),
+        ],
+        compiler_params=pltpu.CompilerParams(
+            collective_id=0, has_side_effects=True, vmem_limit_bytes=48 * 2**20
+        ),
+        name="stacked_ridge",
+    )(dosage, eigvec, eigval, pheno)
+    return jnp.sum(weights, axis=1).reshape(per_device, width)
 
 
 def solution(mesh):

time: 119 us -> 103 us (0.87)
  Pallas kernels: 27.9 us -> 98.4 us
  waiting for transfers between devices: 47.1 us -> 0 us
  other arithmetic: 12.8 us -> 0.02 us
  matrix products: 12.3 us -> 0 us
  local copies, waits for them, and re-layouts: 11.3 us -> 3.99 us
  starting transfers between devices: 6.74 us -> 0 us
    pallas_call x1, Pallas kernels: 27.9 us -> 98.4 us  [on_device(): pl.pallas_call(functools.partial(kernel, regions), out_shape=jax.ShapeDty...]
    all_to_all x1 -> x0, waiting for transfers between devices: 47.1 us -> none  [on_device(): lax.all_to_all(predicted, 'region', split_axis=1, concat_axis=2, tiled=True)]
    dot_general x2 -> x0, matrix products: 12.3 us -> none  [the longest x1 7.31 us: on_device(): lax.dot_general(ridge, std_geno, (((0,), (1,)), ((), ())), preferred_elem...]
    convert_element_type x2 -> x0, other arithmetic: 7.8 us -> none  [the longest x1 4.59 us: on_device(): (rotated[:, None, :] / (eigval[0][:, None, None] + shrink[None, :, None])...]
    all_to_all x1 -> x0, starting transfers between devices: 6.74 us -> none  [on_device(): lax.all_to_all(predicted, 'region', split_axis=1, concat_axis=2, tiled=True)]
    reduce_sum x5 -> x1, other arithmetic: 4.8 us -> 0.02 us  [on_device(): return jnp.sum(weights, axis=1).reshape(per_device, width)]
    reshape x3 -> x1, local copies, waits for them, and re-layouts: 5.27 us -> 0.67 us  [on_device(): return jnp.sum(weights, axis=1).reshape(per_device, width)]
    unnamed x10 -> x6, local copies, waits for them, and re-layouts: 0.56 us -> 3.32 us
  transfers between devices with their start and end apart: 1 -> 0, of which waited for: 1 -> 0; matrix products, arithmetic and copies ran while one was open for 0% -> 0% of each run, Pallas kernels for 0% -> 0%
where the time goes in v2:
time: 103 us; the launch traced here: 102 us
  Pallas kernels  98.4 us (96%)
  local copies, waits for them, and re-layouts  3.99 us (4%)
    pallas_call x1, Pallas kernels, on_device(): pl.pallas_call(functools.partial(kernel, regions), out_shape=jax.ShapeDty...  98.4 us
    unnamed x6, local copies, waits for them, and re-layouts  3.32 us

profile of v2, /device:TPU:13, one launch (start us, length us, event | category | flops | bytes accessed | tf_op | source)
XLA Modules:
  0.0 102.4 jit_solution(9184384163992072643)
XLA Ops:
  0.0 0.0 copy-start
  0.0 1.6 %copy-done = bf16[1024,1024]{1,0:T(8,128)(2,1)S(1)} copy-done((bf16[1024,1024]{1,0:T(8,128)(2,1)S(1)}, bf16[1024,1024]{1,0:T(8,128)(2,1)}, u32[]{:S(2)}) %copy-start) | copy-done | bytes 2097176
  1.6 0.0 copy-start.1
  1.6 1.0 %copy-done.1 = bf16[2048,128]{1,0:T(8,128)(2,1)S(1)} copy-done((bf16[2048,128]{1,0:T(8,128)(2,1)S(1)}, bf16[2048,128]{1,0:T(8,128)(2,1)}, u32[]{:S(2)}) %copy-start.1) | copy-done | bytes 524312
  2.6 0.0 copy-start.2
  2.6 0.7 copy-done.2
  3.3 98.4 %stacked_ridge.1 = f32[2,8,256]{2,1,0:T(8,128)S(1)} custom-call(bf16[2048,1024]{1,0:T(8,128)(2,1)} %dosage_ref.1, bf16[1024,1024]{1,0:T(8,128)(2,1)S(1)} %copy-done, f32[1,1024]{1,0:T(1,128)S(1)} %copy-done.2, bf16[2048,128]{1,0:T(8,128)(2,1)S(1)} %copy-done.1), custom_call_target="tpu_custom_call" | custom-call | tf_op jit(solution)/shard_map/stacked_ridge/pallas_call | solution.py:342
  101.7 0.7 reshape.3
  (1 shorter events, 0.0 us)
Async XLA Ops:
  0.0 1.6 %copy-start = (bf16[1024,1024]{1,0:T(8,128)(2,1)S(1)}, bf16[1024,1024]{1,0:T(8,128)(2,1)}, u32[]{:S(2)}) copy-start(bf16[1024,1024]{1,0:T(8,128)(2,1)} %eigvec_ref.1) | copy-start | bytes 6291460
  1.6 1.0 %copy-start.1 = (bf16[2048,128]{1,0:T(8,128)(2,1)S(1)}, bf16[2048,128]{1,0:T(8,128)(2,1)}, u32[]{:S(2)}) copy-start(bf16[2048,128]{1,0:T(8,128)(2,1)} %pheno_ref.1) | copy-start | bytes 1572868
  2.6 0.7 copy-start.2

commit v3 on v2

--- a/solution.py
+++ b/solution.py
@@ -137,53 +137,27 @@
     )
 
 
-def kernel(
+def level_zero(
     regions,
+    per_chunk,
     dosage_ref,
     eigvec_ref,
     eigval_ref,
     pheno_ref,
-    out_ref,
-    geno_ref,
-    trait_ref,
-    std_trait_ref,
-    cross_ref,
-    wide_ref,
-    scaled_ref,
-    ridge_ref,
-    sent_ref,
-    held_ref,
-    design_ref,
-    target_ref,
-    curve_ref,
-    slope_ref,
-    weight_ref,
-    send_sem,
-    recv_sem,
+    *refs,
 ):
+    *sent_refs, target_ref, geno_ref, trait_ref, std_trait_ref = refs[:-4]
+    cross_ref, wide_ref, scaled_ref, ridge_ref = refs[-4:]
     samples, block = dosage_ref.shape
     traits = pheno_ref.shape[1]
-    sends, _, piece, _ = sent_ref.shape
-    chunks, rows, _ = design_ref.shape
+    sends = len(sent_refs)
+    _, piece, _ = sent_refs[0].shape
     ridges = len(HERITABILITY)
-    width = regions * ridges
-    count = rows // width
+    count = per_chunk
     per_device = traits // regions
     per_send = per_device // sends
     tile = 256
     me = lax.axis_index("region")
-
-    barrier = pltpu.get_barrier_semaphore()
-
-    def greet(k, carry):
-        other = lax.rem(me + k, regions)
-        pl.semaphore_signal(
-            barrier, inc=1, device_id={"region": other}, device_id_type=pl.DeviceIdType.MESH
-        )
-        return carry
-
-    lax.fori_loop(1, regions, greet, 0)
-    pl.semaphore_wait(barrier, regions - 1)
 
     trait = pheno_ref[...].astype(jnp.float32).T
     trait_ref[...] = trait
@@ -254,16 +228,6 @@
 
     lax.fori_loop(0, block // tile, back, 0)
 
-    def copy(send, other, slot):
-        return pltpu.make_async_remote_copy(
-            src_ref=sent_ref.at[send, other],
-            dst_ref=held_ref.at[send, slot],
-            send_sem=send_sem.at[send, other],
-            recv_sem=recv_sem.at[send, slot],
-            device_id={"region": other},
-            device_id_type=pl.DeviceIdType.MESH,
-        )
-
     send_rows = regions * piece
     for send in range(sends):
 
@@ -272,55 +236,39 @@
             part = dot_last(
                 ridge_ref[send * send_rows : (send + 1) * send_rows, :], geno_ref[here, :]
             )
-            part = part.astype(jnp.bfloat16).astype(sent_ref.dtype)
-            sent_ref[send, :, :, here] = part.reshape(regions, piece, tile)
+            part = part.astype(jnp.bfloat16).astype(sent_refs[send].dtype)
+            sent_refs[send][:, :, here] = part.reshape(regions, piece, tile)
             return carry
 
         lax.fori_loop(0, samples // tile, predict, 0)
 
-        def start(k, carry):
-            offset = regions // 2 + (k + 1) // 2 * (1 - 2 * (k % 2))
-            copy(send, lax.rem(me + offset, regions), me).start()
-            return carry
-
-        lax.fori_loop(0, regions - 1, start, 0)
-        held_ref[send, me] = sent_ref[send, me]
-
+
+def level_one(held_ref, target_ref, out_ref, design_ref, curve_ref, slope_ref, weight_ref):
+    regions, piece, samples = held_ref.shape
+    chunks, rows, _ = design_ref.shape
+    ridges = len(HERITABILITY)
+    width = regions * ridges
+    per_send = piece // ridges
+    send_rows = regions * piece
+    tile = 256
     place = lax.broadcasted_iota(jnp.int32, (send_rows, send_rows), 0)
     which = lax.broadcasted_iota(jnp.int32, (send_rows, send_rows), 1)
     wanted = which % per_send * width + which // per_send % ridges * regions + which // piece
     order = jnp.where(place == wanted, 1.0, 0.0).astype(jnp.bfloat16)
-    for send in range(sends):
-
-        def arrive(k, carry):
-            other = lax.rem(me + k, regions)
-            copy(send, other, other).wait_recv()
-            return carry
-
-        lax.fori_loop(1, regions, arrive, 0)
-
-        def sort(i, carry):
-            here = pl.ds(pl.multiple_of(i * tile, tile), tile)
-            part = held_ref[send, :, :, here].reshape(send_rows, tile).astype(jnp.bfloat16)
-            part = jnp.dot(order, part, preferred_element_type=jnp.float32).astype(jnp.bfloat16)
-            design_ref[:, :, here] = part.reshape(chunks, rows, tile)
-            return carry
-
-        lax.fori_loop(0, samples // tile, sort, 0)
-        fit(width, send * chunks, design_ref, target_ref, curve_ref, slope_ref, weight_ref)
-        for chunk in range(chunks):
-            out_ref[send * chunks + chunk] = spread_weights(
-                weight_ref, chunk, width, count, curve_ref.shape[2] // width
-            )
-
-    for send in range(sends):
-
-        def leave(k, carry):
-            other = lax.rem(me + k, regions)
-            copy(send, other, other).wait_send()
-            return carry
-
-        lax.fori_loop(1, regions, leave, 0)
+
+    def sort(i, carry):
+        here = pl.ds(pl.multiple_of(i * tile, tile), tile)
+        part = held_ref[:, :, here].reshape(send_rows, tile).astype(jnp.bfloat16)
+        part = jnp.dot(order, part, preferred_element_type=jnp.float32).astype(jnp.bfloat16)
+        design_ref[:, :, here] = part.reshape(chunks, rows, tile)
+        return carry
+
+    lax.fori_loop(0, samples // tile, sort, 0)
+    fit(width, 0, design_ref, target_ref, curve_ref, slope_ref, weight_ref)
+    for chunk in range(chunks):
+        out_ref[chunk] = spread_weights(
+            weight_ref, chunk, width, rows // width, curve_ref.shape[2] // width
+        )
 
 
 def on_device(dosage, eigvec, eigval, pheno):
@@ -339,11 +287,16 @@
     piece = per_send * ridges
     wire = jnp.bfloat16 if piece % 16 == 0 else jnp.float32
     vmem = pltpu.VMEM
-    weights = pl.pallas_call(
-        functools.partial(kernel, regions),
-        out_shape=jax.ShapeDtypeStruct((sends * chunks, ROWS, count * width), jnp.float32),
-        in_specs=[pl.BlockSpec(memory_space=vmem)] * 4,
-        out_specs=pl.BlockSpec(memory_space=vmem),
+    in_vmem = pl.BlockSpec(memory_space=vmem)
+    params = pltpu.CompilerParams(vmem_limit_bytes=40 * 2**20)
+    *sent, target = pl.pallas_call(
+        functools.partial(level_zero, regions, count),
+        out_shape=[
+            *[jax.ShapeDtypeStruct((regions, piece, samples), wire)] * sends,
+            jax.ShapeDtypeStruct((sends * chunks, ROWS, samples), jnp.float32),
+        ],
+        in_specs=[in_vmem] * 4,
+        out_specs=[in_vmem] * (sends + 1),
         scratch_shapes=[
             vmem((samples, block), jnp.bfloat16),
             vmem((traits, samples), jnp.float32),
@@ -352,22 +305,35 @@
             vmem((traits * ridges, block), jnp.bfloat16),
             vmem((traits * ridges, block), jnp.bfloat16),
             vmem((traits * ridges, block), jnp.bfloat16),
-            vmem((sends, regions, piece, samples), wire),
-            vmem((sends, regions, piece, samples), wire),
-            vmem((chunks, count * width, samples), jnp.bfloat16),
-            vmem((sends * chunks, ROWS, samples), jnp.float32),
-            vmem((groups, width, lanes), jnp.float32),
-            vmem((groups, width, lanes), jnp.float32),
-            vmem((groups, width, lanes), jnp.float32),
-            pltpu.SemaphoreType.DMA((sends, regions)),
-            pltpu.SemaphoreType.DMA((sends, regions)),
         ],
-        compiler_params=pltpu.CompilerParams(
-            collective_id=0, has_side_effects=True, vmem_limit_bytes=48 * 2**20
-        ),
-        name="stacked_ridge",
+        compiler_params=params,
+        name="level_zero",
     )(dosage, eigvec, eigval, pheno)
-    return jnp.sum(weights, axis=1).reshape(per_device, width)
+    held = [
+        lax.all_to_all(sent[send], "region", split_axis=0, concat_axis=0, tiled=True)
+        for send in range(sends)
+    ]
+    weights = [
+        pl.pallas_call(
+            level_one,
+            out_shape=jax.ShapeDtypeStruct((chunks, ROWS, count * width), jnp.float32),
+            in_specs=[in_vmem] * 2,
+            out_specs=in_vmem,
+            scratch_shapes=[
+                vmem((chunks, count * width, samples), jnp.bfloat16),
+                vmem((groups, width, lanes), jnp.float32),
+                vmem((groups, width, lanes), jnp.float32),
+                vmem((groups, width, lanes), jnp.float32),
+            ],
+            compiler_params=params,
+            cost_estimate=pl.CostEstimate(
+                flops=20_000_000_000, bytes_accessed=2**20, transcendentals=0
+            ),
+            name="level_one",
+        )(held[send], target[send * chunks : (send + 1) * chunks])
+        for send in range(sends)
+    ]
+    return jnp.sum(jnp.concatenate(weights), axis=1).reshape(per_device, width)
 
 
 def solution(mesh):

time: 103 us -> 105 us (1.019)
  Pallas kernels: 98.4 us -> 59.9 us
  blocking collectives: 0 us -> 31.2 us
  starting transfers between devices: 0 us -> 5.01 us
  local copies, waits for them, and re-layouts: 3.99 us -> 6.19 us
  waiting for transfers between devices: 0 us -> 1.9 us
    pallas_call x1 -> x3, Pallas kernels: 98.4 us -> 59.9 us  [the longest x2 45.9 us: on_device(): pl.pallas_call(level_one, out_shape=jax.ShapeDtypeStruct((chunks, ROWS, c...]
    all_to_all x0 -> x1, blocking collectives: none -> 31.2 us  [on_device(): lax.all_to_all(sent[send], 'region', split_axis=0, concat_axis=0, tiled=T...]
    all_to_all x0 -> x1, starting transfers between devices: none -> 5.01 us  [on_device(): lax.all_to_all(sent[send], 'region', split_axis=0, concat_axis=0, tiled=T...]
    unnamed x6 -> x8, local copies, waits for them, and re-layouts: 3.32 us -> 5.51 us
    all_to_all x0 -> x1, waiting for transfers between devices: none -> 1.9 us  [on_device(): lax.all_to_all(sent[send], 'region', split_axis=0, concat_axis=0, tiled=T...]
  transfers between devices with their start and end apart: 0 -> 1, of which waited for: 0 -> 1; matrix products, arithmetic and copies ran while one was open for 0% -> 0% of each run, Pallas kernels for 0% -> 22%
where the time goes in v3:
time: 105 us; the launch traced here: 104 us
  Pallas kernels  59.9 us (57%)
  blocking collectives  31.2 us (30%)
  local copies, waits for them, and re-layouts  6.19 us (6%)
  starting transfers between devices  5.01 us (5%)
  waiting for transfers between devices  1.9 us (2%)
    pallas_call x2, Pallas kernels, on_device(): pl.pallas_call(level_one, out_shape=jax.ShapeDtypeStruct((chunks, ROWS, c...  45.9 us
    all_to_all x1, blocking collectives, on_device(): lax.all_to_all(sent[send], 'region', split_axis=0, concat_axis=0, tiled=T...  31.2 us
    pallas_call x1, Pallas kernels, on_device(): pl.pallas_call(functools.partial(level_zero, regions, count), out_shape=[...  13.9 us
    unnamed x8, local copies, waits for them, and re-layouts  5.51 us
    all_to_all x1, starting transfers between devices, on_device(): lax.all_to_all(sent[send], 'region', split_axis=0, concat_axis=0, tiled=T...  5.01 us
  transfers between devices with their start and end apart: 1, of which 1 were waited for; matrix products, arithmetic and copies ran while one was open for 0% of the time, Pallas kernels for 22%

profile of v3, /device:TPU:13, one launch (start us, length us, event | category | flops | bytes accessed | tf_op | source)
XLA Modules:
  0.0 104.2 jit_solution(5874685498073865824)
XLA Ops:
  0.0 0.0 copy-start
  0.0 2.2 %copy-done = bf16[2048,1024]{1,0:T(8,128)(2,1)S(1)} copy-done((bf16[2048,1024]{1,0:T(8,128)(2,1)S(1)}, bf16[2048,1024]{1,0:T(8,128)(2,1)}, u32[]{:S(2)}) %copy-start) | copy-done | bytes 4194328
  2.2 0.0 copy-start.1
  2.2 1.6 %copy-done.1 = bf16[1024,1024]{1,0:T(8,128)(2,1)S(1)} copy-done((bf16[1024,1024]{1,0:T(8,128)(2,1)S(1)}, bf16[1024,1024]{1,0:T(8,128)(2,1)}, u32[]{:S(2)}) %copy-start.1) | copy-done | bytes 2097176
  3.8 0.0 copy-start.2
  3.8 1.0 copy-done.2
  4.8 0.0 copy-start.3
  4.8 0.7 copy-done.3
  5.5 13.9 %level_zero.1 = (bf16[16,16,2048]{2,1,0:T(8,128)(2,1)}, bf16[16,16,2048]{2,1,0:T(8,128)(2,1)S(1)}, f32[2,8,2048]{2,1,0:T(8,128)S(1)}) custom-call(bf16[2048,1024]{1,0:T(8,128)(2,1)S(1)} %copy-done, bf16[1024,1024]{1,0:T(8,128)(2,1)S(1)} %copy-done.1, f32[1,1024]{1,0:T(1,128)S(1)} %copy-done.3, bf16[2048,128]{1,0:T(8,128)(2,1)S(1)} %copy-done.2), custom_call_target="tpu_custom_call" | custom-call | tf_op jit(solution)/shard_map/level_zero/pallas_call | solution.py:292
  19.5 31.2 %all_to_all.10.held_ref = bf16[16,16,2048]{2,1,0:T(8,128)(2,1)S(1)} all-to-all(bf16[16,16,2048]{2,1,0:T(8,128)(2,1)S(1)} %get-tuple-element.10), channel_id=1, replica_groups=mesh['cohort'=2,'region'=16] {'region'}, dimensions={0} | all-to-all | bytes 2097152 | tf_op jit(solution)/shard_map/all_to_all | solution.py:313
  50.6 5.0 %all-to-all-start = ((bf16[16,16,2048]{2,1,0:T(8,128)(2,1)}), bf16[16,16,2048]{2,1,0:T(8,128)(2,1)S(1)}, u32[]{:S(2)}, u32[]{:S(2)}) async-start(bf16[16,16,2048]{2,1,0:T(8,128)(2,1)} %get-tuple-element.8), calls=%async_computation | async-start | bytes 2097152 | tf_op jit(solution)/shard_map/all_to_all | solution.py:313
  55.7 23.0 %level_one.3 = f32[1,8,256]{2,1,0:T(8,128)S(1)} custom-call(bf16[16,16,2048]{2,1,0:T(8,128)(2,1)S(1)} %all_to_all.10.held_ref, f32[1,8,2048]{2,1,0:T(8,128)S(1)} %get-tuple-element.12.target_ref), custom_call_target="tpu_custom_call" | custom-call | flops 20000000000 | bytes 1048576 | tf_op jit(solution)/shard_map/level_one/pallas_call | solution.py:317
  78.6 1.9 %all-to-all-done.held_ref = bf16[16,16,2048]{2,1,0:T(8,128)(2,1)S(1)} async-done(((bf16[16,16,2048]{2,1,0:T(8,128)(2,1)}), bf16[16,16,2048]{2,1,0:T(8,128)(2,1)S(1)}, u32[]{:S(2)}, u32[]{:S(2)}) %all-to-all-start) | async-done | bytes 1048608 | tf_op jit(solution)/shard_map/all_to_all | solution.py:313
  80.5 23.0 %level_one.2 = f32[1,8,256]{2,1,0:T(8,128)S(1)} custom-call(bf16[16,16,2048]{2,1,0:T(8,128)(2,1)S(1)} %all-to-all-done.held_ref, f32[1,8,2048]{2,1,0:T(8,128)S(1)} %get-tuple-element.11.target_ref), custom_call_target="tpu_custom_call" | custom-call | flops 20000000000 | bytes 1048576 | tf_op jit(solution)/shard_map/level_one/pallas_call | solution.py:317
  103.5 0.7 reshape.3
  (2 shorter events, 0.0 us)
Async XLA Ops:
  0.0 2.2 %copy-start = (bf16[2048,1024]{1,0:T(8,128)(2,1)S(1)}, bf16[2048,1024]{1,0:T(8,128)(2,1)}, u32[]{:S(2)}) copy-start(bf16[2048,1024]{1,0:T(8,128)(2,1)} %dosage_ref.1) | copy-start | bytes 12582916
  2.2 1.6 %copy-start.1 = (bf16[1024,1024]{1,0:T(8,128)(2,1)S(1)}, bf16[1024,1024]{1,0:T(8,128)(2,1)}, u32[]{:S(2)}) copy-start(bf16[1024,1024]{1,0:T(8,128)(2,1)} %eigvec_ref.1) | copy-start | bytes 6291460
  3.8 1.0 copy-start.2
  4.8 0.7 copy-start.3
  50.6 29.9 %all-to-all-start = ((bf16[16,16,2048]{2,1,0:T(8,128)(2,1)}), bf16[16,16,2048]{2,1,0:T(8,128)(2,1)S(1)}, u32[]{:S(2)}, u32[]{:S(2)}) async-start(bf16[16,16,2048]{2,1,0:T(8,128)(2,1)} %get-tuple-element.8), calls=%async_computation | async-start | bytes 2097152 | tf_op jit(solution)/shard_map/all_to_all | solution.py:313

commit v4 on v3

--- a/solution.py
+++ b/solution.py
@@ -37,7 +37,9 @@
         for j in range(ROWS):
             for g in range(groups):
                 column = pick_column(curves[g], first + j, width)
-                inverse = 1.0 / column[j : j + 1, :]
+                inverse = pl.reciprocal(column[j : j + 1, :], approx=True)
+                inverse = inverse * (2.0 - column[j : j + 1, :] * inverse)
+                inverse = inverse * (2.0 - column[j : j + 1, :] * inverse)
                 pivot = curves[g][j : j + 1, :] * inverse
                 right = slopes[g][j : j + 1, :] * inverse
                 curves[g] = jnp.where(row == j, pivot, curves[g] - column * pivot)
@@ -280,7 +282,7 @@
     width = regions * ridges
     lanes = max(width, LANES)
     count = max(1, 2 * LANES // width)
-    per_send = max(count, min(per_device, 2))
+    per_send = per_device
     sends = per_device // per_send
     chunks = per_send // count
     groups = per_send * width // lanes

time: 105 us -> 106 us (level); the launches traced: 104 us -> 104 us
  blocking collectives: 31.2 us -> 53.7 us
  Pallas kernels: 59.9 us -> 44.2 us
  starting transfers between devices: 5.01 us -> 0 us
  waiting for transfers between devices: 1.9 us -> 0 us
    all_to_all x1, blocking collectives: 31.2 us -> 53.7 us  [on_device(): lax.all_to_all(sent[send], 'region', split_axis=0, concat_axis=0, tiled=T...]
    pallas_call x2 -> x1, Pallas kernels: 45.9 us -> 32.5 us  [on_device(): pl.pallas_call(level_one, out_shape=jax.ShapeDtypeStruct((chunks, ROWS, c...]
    all_to_all x1 -> x0, starting transfers between devices: 5.01 us -> none  [on_device(): lax.all_to_all(sent[send], 'region', split_axis=0, concat_axis=0, tiled=T...]
    pallas_call x1, Pallas kernels: 13.9 us -> 11.7 us  [on_device(): pl.pallas_call(functools.partial(level_zero, regions, count), out_shape=[...]
    all_to_all x1 -> x0, waiting for transfers between devices: 1.9 us -> none  [on_device(): lax.all_to_all(sent[send], 'region', split_axis=0, concat_axis=0, tiled=T...]
  transfers between devices with their start and end apart: 1 -> 0, of which waited for: 1 -> 0; matrix products, arithmetic and copies ran while one was open for 0% -> 0% of each run, Pallas kernels for 22% -> 0%
where the time goes in v4:
time: 106 us; the launch traced here: 104 us
  blocking collectives  53.7 us (51%)
  Pallas kernels  44.2 us (42%)
  local copies, waits for them, and re-layouts  6.18 us (6%)
    all_to_all x1, blocking collectives, on_device(): lax.all_to_all(sent[send], 'region', split_axis=0, concat_axis=0, tiled=T...  53.7 us
    pallas_call x1, Pallas kernels, on_device(): pl.pallas_call(level_one, out_shape=jax.ShapeDtypeStruct((chunks, ROWS, c...  32.5 us
    pallas_call x1, Pallas kernels, on_device(): pl.pallas_call(functools.partial(level_zero, regions, count), out_shape=[...  11.7 us
    unnamed x8, local copies, waits for them, and re-layouts  5.51 us

profile of v4, /device:TPU:13, one launch (start us, length us, event | category | flops | bytes accessed | tf_op | source)
XLA Modules:
  0.0 104.1 jit_solution(14665809228144588318)
XLA Ops:
  0.0 0.0 copy-start
  0.0 2.2 %copy-done = bf16[2048,1024]{1,0:T(8,128)(2,1)S(1)} copy-done((bf16[2048,1024]{1,0:T(8,128)(2,1)S(1)}, bf16[2048,1024]{1,0:T(8,128)(2,1)}, u32[]{:S(2)}) %copy-start) | copy-done | bytes 4194328
  2.2 0.0 copy-start.1
  2.2 1.6 %copy-done.1 = bf16[1024,1024]{1,0:T(8,128)(2,1)S(1)} copy-done((bf16[1024,1024]{1,0:T(8,128)(2,1)S(1)}, bf16[1024,1024]{1,0:T(8,128)(2,1)}, u32[]{:S(2)}) %copy-start.1) | copy-done | bytes 2097176
  3.8 0.0 copy-start.2
  3.8 1.0 copy-done.2
  4.8 0.0 copy-start.3
  4.8 0.7 copy-done.3
  5.5 11.7 %level_zero.1 = (bf16[16,32,2048]{2,1,0:T(8,128)(2,1)S(1)}, f32[2,8,2048]{2,1,0:T(8,128)S(1)}) custom-call(bf16[2048,1024]{1,0:T(8,128)(2,1)S(1)} %copy-done, bf16[1024,1024]{1,0:T(8,128)(2,1)S(1)} %copy-done.1, f32[1,1024]{1,0:T(1,128)S(1)} %copy-done.3, bf16[2048,128]{1,0:T(8,128)(2,1)S(1)} %copy-done.2), custom_call_target="tpu_custom_call" | custom-call | tf_op jit(solution)/shard_map/level_zero/pallas_call | solution.py:294
  17.2 53.7 %all_to_all.5.held_ref = bf16[16,32,2048]{2,1,0:T(8,128)(2,1)S(1)} all-to-all(bf16[16,32,2048]{2,1,0:T(8,128)(2,1)S(1)} %get-tuple-element.7), channel_id=1, replica_groups=mesh['cohort'=2,'region'=16] {'region'}, dimensions={0} | all-to-all | bytes 4194304 | tf_op jit(solution)/shard_map/all_to_all | solution.py:315
  70.9 32.5 %level_one.1 = f32[2,8,256]{2,1,0:T(8,128)S(1)} custom-call(bf16[16,32,2048]{2,1,0:T(8,128)(2,1)S(1)} %all_to_all.5.held_ref, f32[2,8,2048]{2,1,0:T(8,128)S(1)} %get-tuple-element.8.target_ref), custom_call_target="tpu_custom_call" | custom-call | flops 20000000000 | bytes 1048576 | tf_op jit(solution)/shard_map/level_one/pallas_call | solution.py:319
  103.4 0.7 reshape.3
  (1 shorter events, 0.0 us)
Async XLA Ops:
  0.0 2.2 %copy-start = (bf16[2048,1024]{1,0:T(8,128)(2,1)S(1)}, bf16[2048,1024]{1,0:T(8,128)(2,1)}, u32[]{:S(2)}) copy-start(bf16[2048,1024]{1,0:T(8,128)(2,1)} %dosage_ref.1) | copy-start | bytes 12582916
  2.2 1.6 %copy-start.1 = (bf16[1024,1024]{1,0:T(8,128)(2,1)S(1)}, bf16[1024,1024]{1,0:T(8,128)(2,1)}, u32[]{:S(2)}) copy-start(bf16[1024,1024]{1,0:T(8,128)(2,1)} %eigvec_ref.1) | copy-start | bytes 6291460
  3.8 1.0 %copy-start.2 = (bf16[2048,128]{1,0:T(8,128)(2,1)S(1)}, bf16[2048,128]{1,0:T(8,128)(2,1)}, u32[]{:S(2)}) copy-start(bf16[2048,128]{1,0:T(8,128)(2,1)} %pheno_ref.1) | copy-start | bytes 1572868
  4.8 0.7 copy-start.3
